TPU v7x, 32 devices: a whole 2x2x4 slice. The times are simulated.
32 devices in a mesh: dp: 8 (over y, x, core), tensor: 4 (over z).
Axes of the slice: x: 2, y: 2, z: 4, core: 2. Of those that a mesh axis runs over, the one named last changes fastest.
Arguments:
- inputs: bfloat16 [2, 4096, 1120], P(None, ('dp', 'tensor')), may hold values from -6 to 6
- segments: int32 [2, 4096], P(None, ('dp', 'tensor')), may hold values from -1 to 4, as said below
- norm1_gain: float32 [1120], replicated, may hold values from 0.1 to 1.9
- norm1_bias: float32 [1120], replicated, may hold values from -1.75 to 1.75
- qkv_weight: bfloat16 [3, 1120, 1120], P(None, None, 'tensor'), may hold values from -0.1875 to 0.1875
- out_weight: bfloat16 [1120, 1120], P('tensor'), may hold values from -1.5 to 1.5
- norm2_gain: float32 [1120], replicated, may hold values from 0.1 to 1.9
- norm2_bias: float32 [1120], replicated, may hold values from -1.75 to 1.75
- up_weight: bfloat16 [1120, 4480], P(None, 'tensor'), may hold values from -0.1875 to 0.1875
- down_weight: bfloat16 [4480, 1120], P('tensor'), may hold values from -0.09375 to 0.09375
- cotangent: bfloat16 [2, 4096, 1120], P(None, ('dp', 'tensor')), may hold values from -6 to 6
Outputs:
- output: bfloat16 [2, 4096, 1120], P(None, ('dp', 'tensor'))
- input_grad: float32 [2, 4096, 1120], P(None, ('dp', 'tensor'))
- norm1_gain_grad: float32 [1120], replicated
- norm1_bias_grad: float32 [1120], replicated
- qkv_grad: float32 [3, 1120, 1120], P(None, None, 'tensor')
- out_grad: float32 [1120, 1120], P('tensor')
- norm2_gain_grad: float32 [1120], replicated
- norm2_bias_grad: float32 [1120], replicated
- up_grad: float32 [1120, 4480], P(None, 'tensor')
- down_grad: float32 [4480, 1120], P('tensor')
Inputs may be any that keep to these rules, and one draw needn't show every extreme that they name: `segments`: in each row, cell 0 starts at the row's first token and holds more than three quarters of the row; the row ends with one or more padding tokens (-1); between them cell numbers rise by one from cell to cell, each cell of consecutive tokens.
All inputs are finite; a program needn't handle non-finite values.
Results may differ from a plain program's by a relative error of at most 0.015.
Values may be sent and summed in bfloat16 or wider, within the bound.
A program may use at most 128 MiB of HBM per device.

v0:
```python
import jax
import jax.numpy as jnp
from jax import lax
from jax.sharding import PartitionSpec as P

HD = 56


def layer_norm(values, gain, shift):
    center = values - jnp.mean(values, axis=-1, keepdims=True)
    spread = jnp.mean(center * center, axis=-1, keepdims=True)
    return center * lax.rsqrt(spread + 1e-05) * gain + shift


def gelu_tanh(values):
    return jax.nn.gelu(values, approximate=True)


def shards(
    inputs,
    segments,
    norm1_gain,
    norm1_bias,
    qkv_weight,
    out_weight,
    norm2_gain,
    norm2_bias,
    up_weight,
    down_weight,
    cotangent,
):
    shard_rows = inputs.shape[1]
    local_width = qkv_weight.shape[2]
    local_heads = local_width // HD
    full_rows = shard_rows * lax.axis_size("tensor")
    score_scale = HD ** (-0.5)
    micro_count = inputs.shape[0]
    all_labels = lax.all_gather(segments, "tensor", axis=1, tiled=True)
    places = jnp.arange(full_rows, dtype=jnp.int32)
    causal = places[:, None] >= places[None, :]
    grad_qkv = jnp.zeros(qkv_weight.shape, jnp.float32)
    grad_out_weight = jnp.zeros(out_weight.shape, jnp.float32)
    grad_up = jnp.zeros(up_weight.shape, jnp.float32)
    grad_down = jnp.zeros(down_weight.shape, jnp.float32)
    gain_one = jnp.zeros_like(norm1_gain)
    shift_one = jnp.zeros_like(norm1_bias)
    gain_two = jnp.zeros_like(norm2_gain)
    shift_two = jnp.zeros_like(norm2_bias)
    outputs = []
    input_grads = []
    for micro_step in range(micro_count):
        residual_in = inputs[micro_step].astype(jnp.float32)
        norm_one, ln_one_back = jax.vjp(layer_norm, residual_in, norm1_gain, norm1_bias)
        norm_one = norm_one.astype(jnp.bfloat16)
        gathered_one = lax.all_gather(norm_one, "tensor", axis=0, tiled=True)
        projected = jnp.einsum(
            "td,cdf->ctf", gathered_one, qkv_weight, preferred_element_type=jnp.float32
        ).astype(jnp.bfloat16)
        queries = projected[0].reshape(full_rows, local_heads, HD)
        keys = projected[1].reshape(full_rows, local_heads, HD)
        values = projected[2].reshape(full_rows, local_heads, HD)
        labels = all_labels[micro_step]
        allowed = causal & (labels[:, None] == labels[None, :])
        scores = (
            jnp.einsum("qhe,khe->hqk", queries, keys, preferred_element_type=jnp.float32)
            * score_scale
        )
        scores = jnp.where(allowed[None], scores, -1e30)
        row_peak = jnp.max(scores, axis=-1, keepdims=True)
        expo = jnp.exp(scores - row_peak)
        row_total = jnp.sum(expo, axis=-1, keepdims=True)
        log_total = row_peak + jnp.log(row_total)
        probs_low = (expo / row_total).astype(jnp.bfloat16)
        heads_out = jnp.einsum(
            "hqk,khe->qhe", probs_low, values, preferred_element_type=jnp.float32
        )
        heads_out = heads_out.astype(jnp.bfloat16).reshape(full_rows, local_width)
        attn = lax.psum_scatter(
            jnp.dot(heads_out, out_weight, preferred_element_type=jnp.float32),
            "tensor",
            scatter_dimension=0,
            tiled=True,
        )
        resid = residual_in + attn
        norm_two, ln_two_back = jax.vjp(layer_norm, resid, norm2_gain, norm2_bias)
        norm_two = norm_two.astype(jnp.bfloat16)
        gathered_two = lax.all_gather(norm_two, "tensor", axis=0, tiled=True)
        hidden_in = jnp.dot(gathered_two, up_weight, preferred_element_type=jnp.float32)
        activated, gelu_back = jax.vjp(gelu_tanh, hidden_in)
        hidden = activated.astype(jnp.bfloat16)
        branch = lax.psum_scatter(
            jnp.dot(hidden, down_weight, preferred_element_type=jnp.float32).astype(jnp.bfloat16),
            "tensor",
            scatter_dimension=0,
            tiled=True,
        ).astype(jnp.float32)
        outputs.append((resid + branch).astype(jnp.bfloat16))
        live_mask = (segments[micro_step] >= 0)[:, None].astype(jnp.float32)
        grad_final = cotangent[micro_step].astype(jnp.float32) * live_mask
        grad_branch = lax.all_gather(grad_final.astype(jnp.bfloat16), "tensor", axis=0, tiled=True)
        grad_down = grad_down + jnp.einsum(
            "tf,td->fd", hidden, grad_branch, preferred_element_type=jnp.float32
        )
        grad_hidden = jnp.einsum(
            "td,fd->tf", grad_branch, down_weight, preferred_element_type=jnp.float32
        )
        up_grad_in = gelu_back(grad_hidden)[0].astype(jnp.bfloat16)
        grad_up = grad_up + jnp.einsum(
            "td,tf->df", gathered_two, up_grad_in, preferred_element_type=jnp.float32
        )
        grad_norm_two = lax.psum_scatter(
            jnp.einsum("tf,df->td", up_grad_in, up_weight, preferred_element_type=jnp.float32),
            "tensor",
            scatter_dimension=0,
            tiled=True,
        )
        resid_back, gain_piece, shift_piece = ln_two_back(grad_norm_two)
        gain_two = gain_two + gain_piece
        shift_two = shift_two + shift_piece
        grad_resid = grad_final + resid_back
        grad_attn = lax.all_gather(grad_resid.astype(jnp.bfloat16), "tensor", axis=0, tiled=True)
        grad_out_weight = grad_out_weight + jnp.einsum(
            "tc,td->cd", heads_out, grad_attn, preferred_element_type=jnp.float32
        )
        grad_heads = jnp.einsum(
            "td,cd->tc", grad_attn, out_weight, preferred_element_type=jnp.float32
        )
        grad_heads = grad_heads.astype(jnp.bfloat16).reshape(full_rows, local_heads, HD)
        again_scores = (
            jnp.einsum("qhe,khe->hqk", queries, keys, preferred_element_type=jnp.float32)
            * score_scale
        )
        again_scores = jnp.where(allowed[None], again_scores, -1e30)
        probs = jnp.exp(again_scores - log_total)
        probs_again = probs.astype(jnp.bfloat16)
        grad_probs = jnp.einsum(
            "qhe,khe->hqk", grad_heads, values, preferred_element_type=jnp.float32
        )
        row_delta = jnp.sum(probs * grad_probs, axis=-1, keepdims=True)
        grad_scores = (probs * (grad_probs - row_delta)).astype(jnp.bfloat16)
        grad_queries = (
            jnp.einsum("hqk,khe->qhe", grad_scores, keys, preferred_element_type=jnp.float32)
            * score_scale
        )
        grad_keys = (
            jnp.einsum("hqk,qhe->khe", grad_scores, queries, preferred_element_type=jnp.float32)
            * score_scale
        )
        grad_values = jnp.einsum(
            "hqk,qhe->khe", probs_again, grad_heads, preferred_element_type=jnp.float32
        )
        grad_projected = (
            jnp.stack([grad_queries, grad_keys, grad_values])
            .reshape(3, full_rows, local_width)
            .astype(jnp.bfloat16)
        )
        grad_qkv = grad_qkv + jnp.einsum(
            "td,ctf->cdf", gathered_one, grad_projected, preferred_element_type=jnp.float32
        )
        grad_norm_one = lax.psum_scatter(
            jnp.einsum(
                "ctf,cdf->td", grad_projected, qkv_weight, preferred_element_type=jnp.float32
            ).astype(jnp.bfloat16),
            "tensor",
            scatter_dimension=0,
            tiled=True,
        ).astype(jnp.float32)
        input_back, gain_piece, shift_piece = ln_one_back(grad_norm_one)
        gain_one = gain_one + gain_piece
        shift_one = shift_one + shift_piece
        input_grads.append(grad_resid + input_back)
    grad_qkv, grad_out_weight, grad_up, grad_down = lax.psum(
        (grad_qkv, grad_out_weight, grad_up, grad_down), "dp"
    )
    gain_one, shift_one, gain_two, shift_two = lax.psum(
        (gain_one, shift_one, gain_two, shift_two), ("dp", "tensor")
    )
    return (
        jnp.stack(outputs),
        jnp.stack(input_grads),
        gain_one,
        shift_one,
        grad_qkv,
        grad_out_weight,
        gain_two,
        shift_two,
        grad_up,
        grad_down,
    )


def solution(mesh):
    return jax.shard_map(
        shards,
        mesh=mesh,
        in_specs=(
            P(None, ("dp", "tensor"), None),
            P(None, ("dp", "tensor")),
            P(),
            P(),
            P(None, None, "tensor"),
            P("tensor", None),
            P(),
            P(),
            P(None, "tensor"),
            P("tensor", None),
            P(None, ("dp", "tensor"), None),
        ),
        out_specs=(
            P(None, ("dp", "tensor"), None),
            P(None, ("dp", "tensor"), None),
            P(),
            P(),
            P(None, None, "tensor"),
            P("tensor", None),
            P(),
            P(),
            P(None, "tensor"),
            P("tensor", None),
        ),
        check_vma=False,
    )
```

profile of v0, /device:TPU:0, one launch (start us, length us, event | category | flops | bytes accessed | tf_op | source)
XLA Modules:
  0.0 822.8 jit_solution(1636673675468683847)
XLA Ops:
  7.2 1.4 convert_reduce_fusion.3
  8.6 1.2 fusion.70
  10.3 2.3 fusion.69
  13.4 12.6 %all_gather.28 = s32[2,512]{1,0:T(2,128)S(1)} all-gather(s32[2,128]{1,0:T(2,128)S(1)} %copy-done.78), channel_id=1, replica_groups=mesh['dp'=8,'tensor'=4] {'tensor'}, dimensions={1}, use_global_device_ids=true | all-gather | bytes 5120 | tf_op jit(solution)/shard_map/all_gather | solution.py:38
  26.2 20.7 %all-gather.9.cloned.1.call-done = bf16[512,1120]{0,1:T(8,128)(2,1)} async-done(((bf16[128,1120]{0,1:T(8,128)(2,1)}), bf16[512,1120]{0,1:T(8,128)(2,1)}) %all-gather.9.cloned.1.call-update) | async-done | bytes 1146896 | tf_op jit(solution)/shard_map/all_gather | solution.py:55
  47.0 3.2 fusion.29
  52.1 1.5 copy-done.3
  55.3 2.2 fusion.108
  58.5 20.4 %all-gather.13.cloned.1.call-done = bf16[512,1120]{0,1:T(8,128)(2,1)} async-done(((bf16[128,1120]{0,1:T(8,128)(2,1)}), bf16[512,1120]{0,1:T(8,128)(2,1)}) %all-gather.13.cloned.1.call-update) | async-done | bytes 1146896 | tf_op jit(solution)/shard_map/all_gather | solution.py:55
  78.9 3.2 fusion.30
  84.1 1.6 copy-done.2
  87.5 2.2 fusion.109
  90.4 2.0 fusion.79
  92.4 34.8 %reduce-scatter.17.cloned.1.call-done = f32[128,1120]{0,1:T(8,128)} async-done(((f32[512,1120]{0,1:T(8,128)}), f32[128,1120]{0,1:T(8,128)}) %reduce-scatter.17.cloned.1.call-update) | async-done | bytes 573456 | tf_op jit(solution)/shard_map/reduce_scatter | solution.py:78
  127.2 49.3 %reduce-scatter.19.cloned.1.call-done = f32[128,1120]{0,1:T(8,128)} async-done(((f32[512,1120]{0,1:T(8,128)}), f32[128,1120]{0,1:T(8,128)}) %reduce-scatter.19.cloned.1.call-update) | async-done | bytes 573456 | tf_op jit(solution)/shard_map/reduce_scatter | solution.py:78
  176.6 1.4 fusion.99
  182.2 27.3 %all-gather.21.cloned.1.call-done = bf16[512,1120]{0,1:T(8,128)(2,1)} async-done(((bf16[128,1120]{0,1:T(8,128)(2,1)}), bf16[512,1120]{0,1:T(8,128)(2,1)}) %all-gather.21.cloned.1.call-update) | async-done | bytes 1146896 | tf_op jit(solution)/shard_map/all_gather | solution.py:100
  209.5 5.1 fusion.114
  214.6 26.7 %all-gather.15.cloned.1.call-done = bf16[512,1120]{0,1:T(8,128)(2,1)} async-done(((bf16[128,1120]{0,1:T(8,128)(2,1)}), bf16[512,1120]{0,1:T(8,128)(2,1)}) %all-gather.15.cloned.1.call-update) | async-done | bytes 1146896 | tf_op jit(solution)/shard_map/all_gather | solution.py:87
  241.3 6.2 fusion.28
  247.5 1.4 copy-done.22
  248.9 2.8 convolution_convert_fusion
  251.7 2.4 copy.47
  254.1 19.2 %all-gather.17.cloned.1.call-done = bf16[512,1120]{0,1:T(8,128)(2,1)} async-done(((bf16[128,1120]{0,1:T(8,128)(2,1)}), bf16[512,1120]{0,1:T(8,128)(2,1)}) %all-gather.17.cloned.1.call-update) | async-done | bytes 1146896 | tf_op jit(solution)/shard_map/all_gather | solution.py:100
  273.3 5.1 fusion.112
  278.4 26.9 %all-gather.11.cloned.1.call-done = bf16[512,1120]{0,1:T(8,128)(2,1)} async-done(((bf16[128,1120]{0,1:T(8,128)(2,1)}), bf16[512,1120]{0,1:T(8,128)(2,1)}) %all-gather.11.cloned.1.call-update) | async-done | bytes 1146896 | tf_op jit(solution)/shard_map/all_gather | solution.py:87
  305.3 6.1 fusion.21
  311.4 1.4 copy-done.97
  312.8 2.8 convolution_convert_fusion.1
  315.6 2.4 copy.45
  318.3 4.3 fusion.113
  322.6 4.3 fusion.115
  327.1 8.1 reduce-scatter.27.cloned.1.call-done
  336.3 29.5 %reduce-scatter.25.cloned.1.call-done = bf16[128,1120]{1,0:T(8,128)(2,1)} async-done(((bf16[512,1120]{1,0:T(8,128)(2,1)}), bf16[128,1120]{1,0:T(8,128)(2,1)}) %reduce-scatter.25.cloned.1.call-update) | async-done | bytes 286736
  365.8 1.8 copy.46
  367.6 46.8 %reduce-scatter.21.cloned.1.call-done = f32[128,1120]{0,1:T(8,128)} async-done(((f32[512,1120]{0,1:T(8,128)}), f32[128,1120]{0,1:T(8,128)}) %reduce-scatter.21.cloned.1.call-update) | async-done | bytes 573456 | tf_op jit(solution)/shard_map/reduce_scatter | solution.py:111
  414.5 49.4 %reduce-scatter.23.cloned.1.call-done = f32[128,1120]{0,1:T(8,128)} async-done(((f32[512,1120]{0,1:T(8,128)}), f32[128,1120]{0,1:T(8,128)}) %reduce-scatter.23.cloned.1.call-update) | async-done | bytes 573456 | tf_op jit(solution)/shard_map/reduce_scatter | solution.py:111
  463.9 2.2 multiply_reduce_fusion.3
  466.2 2.0 fusion.97
  470.2 3.1 fusion.111
  473.3 4.0 convolution_add_fusion.1
  477.6 23.5 %all-gather.19.cloned.1.call-done = bf16[512,1120]{0,1:T(8,128)(2,1)} async-done(((bf16[128,1120]{0,1:T(8,128)(2,1)}), bf16[512,1120]{0,1:T(8,128)(2,1)}) %all-gather.19.cloned.1.call-update) | async-done | bytes 1146896 | tf_op jit(solution)/shard_map/all_gather | solution.py:121
  501.1 1.8 convolution_convert_fusion.5
  503.0 3.8 multiply_reduce_fusion.1
  507.0 1.5 multiply_convert_fusion.1
  511.6 2.4 fusion.5
  514.0 2.4 copy.49
  516.8 17.3 %all-gather.23.cloned.1.call-done = bf16[512,1120]{0,1:T(8,128)(2,1)} async-done(((bf16[128,1120]{0,1:T(8,128)(2,1)}), bf16[512,1120]{0,1:T(8,128)(2,1)}) %all-gather.23.cloned.1.call-update) | async-done | bytes 1146896 | tf_op jit(solution)/shard_map/all_gather | solution.py:121
  534.0 1.8 convolution_convert_fusion.4
  535.8 3.7 multiply_reduce_fusion
  540.1 1.5 multiply_convert_fusion
  544.6 2.4 fusion.6
  547.0 2.4 copy.51
  549.8 4.2 fusion.96
  554.1 4.2 convolution_add_fusion
  559.6 1.6 convolution_add_fusion.3
  561.3 1.3 fusion.45
  562.7 3.3 fusion.4
  569.1 23.3 %reduce-scatter.31.cloned.1.call-done = bf16[128,1120]{1,0:T(8,128)(2,1)} async-done(((bf16[512,1120]{1,0:T(8,128)(2,1)}), bf16[128,1120]{1,0:T(8,128)(2,1)}) %reduce-scatter.31.cloned.1.call-update) | async-done | bytes 286736
  595.0 40.8 %all-reduce = (f32[1120]{0:T(1024)}, f32[1120]{0:T(1024)}, f32[1120]{0:T(1024)}, f32[1120]{0:T(1024)}) all-reduce(f32[1120]{0:T(1024)S(1)} %add.205, f32[1120]{0:T(1024)S(1)} %add.206, f32[1120]{0:T(1024)S(1)} %add.210, f32[1120]{0:T(1024)S(1)} %add.211), channel_id=1, replica_groups=mesh['dp'=8,'tensor'=4] {'dp','tensor'}, use_global_device_ids=true, to_apply=%region_32.33 | all-reduce | flops 4480 | bytes 35840 | tf_op jit(solution)/shard_map/psum | solution.py:175
  637.5 165.4 %all-reduce.4.cloned.1.call-done = (f32[3,1120,280]{1,2,0:T(8,128)}, f32[280,1120]{1,0:T(8,128)}, f32[1120,1120]{1,0:T(8,128)}, f32[1120,1120]{1,0:T(8,128)}) async-done(((f32[3,1120,280]{1,2,0:T(8,128)}, f32[280,1120]{1,0:T(8,128)}, f32[1120,1120]{1,0:T(8,128)}, f32[1120,1120]{1,0:T(8,128)}), (f32[3,1120,280]{1,2,0:T(8,128)}, f32[280,1120]{1,0:T(8,128)}, f32[1120,1120]{1,0:T(8,128)}, ...) | async-done | bytes 15052816 | tf_op jit(solution)/shard_map/psum | solution.py:172
  803.0 4.4 copy.57
  808.5 2.6 copy.59
  812.2 2.6 copy.60
  (296 shorter events, 37.8 us)
Async XLA Ops:
  7.2 234.2 %copy-start = (bf16[1120,1120]{1,0:T(8,128)(2,1)S(1)}, bf16[1120,1120]{1,0:T(8,128)(2,1)}, u32[]{:S(2)}) copy-start(bf16[1120,1120]{1,0:T(8,128)(2,1)} %param.19) | copy-start | bytes 7526404
  7.2 6.2 copy-start.78
  7.2 39.7 %all-gather.9.cloned.1.call-start = ((), (), s32[]{:S(2)}) async-start(), calls=%async_computation.8 | async-start | bytes 1433600 | tf_op jit(solution)/shard_map/all_gather | solution.py:55
  9.8 40.3 %copy-start.83 = (f32[128]{0:T(128)}, f32[128]{0:T(128)S(1)}, u32[]{:S(2)}) copy-start(f32[128]{0:T(128)S(1)} %get-tuple-element.25) | copy-start | bytes 1540
  10.3 36.6 %copy-start.72 = (f32[128]{0:T(128)}, f32[128]{0:T(128)S(1)}, u32[]{:S(2)}) copy-start(f32[128]{0:T(128)S(1)} %fusion.88) | copy-start | bytes 1540
  10.3 36.6 %copy-start.70 = (f32[128]{0:T(128)}, f32[128]{0:T(128)S(1)}, u32[]{:S(2)}) copy-start(f32[128]{0:T(128)S(1)} %fusion.90) | copy-start | bytes 1540
  12.6 66.3 %all-gather.13.cloned.1.call-start = ((), (), s32[]{:S(2)}) async-start(), calls=%async_computation.11 | async-start | bytes 1433600 | tf_op jit(solution)/shard_map/all_gather | solution.py:55
  13.3 113.9 %reduce-scatter.17.cloned.1.call-start = ((), (), s32[]{:S(2)}) async-start(), calls=%async_computation.9 | async-start | bytes 2867200 | tf_op jit(solution)/shard_map/reduce_scatter | solution.py:78
  57.6 119.0 %reduce-scatter.19.cloned.1.call-start = ((), (), s32[]{:S(2)}) async-start(), calls=%async_computation.12 | async-start | bytes 2867200 | tf_op jit(solution)/shard_map/reduce_scatter | solution.py:78
  89.7 86.9 %copy-start.4 = (bf16[2,128,1120]{1,2,0:T(8,128)(2,1)S(1)}, bf16[2,128,1120]{1,2,0:T(8,128)(2,1)}, u32[]{:S(2)}) copy-start(bf16[2,128,1120]{1,2,0:T(8,128)(2,1)} %param.11) | copy-start | bytes 1720324
  89.7 119.8 %all-gather.21.cloned.1.call-start = ((), (), s32[]{:S(2)}) async-start(), calls=%async_computation.17 | async-start | bytes 1433600 | tf_op jit(solution)/shard_map/all_gather | solution.py:100
  92.3 86.6 %copy-start.58 = (f32[1120]{0:T(1024)S(1)}, f32[1120]{0:T(1024)}, u32[]{:S(2)}) copy-start(f32[1120]{0:T(1024)} %param.17) | copy-start | bytes 13444
  92.3 86.7 %copy-start.59 = (f32[1120]{0:T(1024)S(1)}, f32[1120]{0:T(1024)}, u32[]{:S(2)}) copy-start(f32[1120]{0:T(1024)} %param.18) | copy-start | bytes 13444
  92.3 149.0 %all-gather.15.cloned.1.call-start = ((), (), s32[]{:S(2)}) async-start(), calls=%async_computation.13 | async-start | bytes 1433600 | tf_op jit(solution)/shard_map/all_gather | solution.py:87
  178.0 36.6 %copy-start.66 = (f32[128]{0:T(128)}, f32[128]{0:T(128)S(1)}, u32[]{:S(2)}) copy-start(f32[128]{0:T(128)S(1)} %broadcast_multiply_fusion) | copy-start | bytes 1540
  178.2 36.4 %copy-start.68 = (f32[128]{0:T(128)}, f32[128]{0:T(128)S(1)}, u32[]{:S(2)}) copy-start(f32[128]{0:T(128)S(1)} %broadcast_multiply_fusion.2) | copy-start | bytes 1540
  178.9 35.7 %copy-start.89 = (f32[128]{0:T(128)}, f32[128]{0:T(128)S(1)}, u32[]{:S(2)}) copy-start(f32[128]{0:T(128)S(1)} %multiply_reduce_fusion.7) | copy-start | bytes 1540
  178.9 35.7 %copy-start.74 = (f32[128]{0:T(128)}, f32[128]{0:T(128)S(1)}, u32[]{:S(2)}) copy-start(f32[128]{0:T(128)S(1)} %fusion.91) | copy-start | bytes 1540
  179.0 35.6 %copy-start.76 = (f32[128]{0:T(128)}, f32[128]{0:T(128)S(1)}, u32[]{:S(2)}) copy-start(f32[128]{0:T(128)S(1)} %fusion.89) | copy-start | bytes 1540
  180.2 93.1 %all-gather.17.cloned.1.call-start = ((), (), s32[]{:S(2)}) async-start(), calls=%async_computation.14 | async-start | bytes 1433600 | tf_op jit(solution)/shard_map/all_gather | solution.py:100
  180.9 124.3 %all-gather.11.cloned.1.call-start = ((), (), s32[]{:S(2)}) async-start(), calls=%async_computation.10 | async-start | bytes 1433600 | tf_op jit(solution)/shard_map/all_gather | solution.py:87
  181.7 153.4 %reduce-scatter.27.cloned.1.call-start = ((), (), s32[]{:S(2)}) async-start(), calls=%async_computation.21 | async-start | bytes 1474560
  241.3 7.5 copy-start.91
  254.1 111.7 %reduce-scatter.25.cloned.1.call-start = ((), (), s32[]{:S(2)}) async-start(), calls=%async_computation.20 | async-start | bytes 1474560
  305.3 7.5 copy-start.92
  318.0 96.4 %reduce-scatter.21.cloned.1.call-start = ((), (), s32[]{:S(2)}) async-start(), calls=%async_computation.15 | async-start | bytes 2867200 | tf_op jit(solution)/shard_map/reduce_scatter | solution.py:111
  322.6 141.2 %reduce-scatter.23.cloned.1.call-start = ((), (), s32[]{:S(2)}) async-start(), calls=%async_computation.18 | async-start | bytes 2867200 | tf_op jit(solution)/shard_map/reduce_scatter | solution.py:111
  326.9 136.9 %copy-start.6 = (f32[128,1120]{0,1:T(8,128)S(1)}, f32[128,1120]{0,1:T(8,128)}, u32[]{:S(2)}) copy-start(f32[128,1120]{0,1:T(8,128)} %copy-done.5) | copy-start | bytes 1720324
  326.9 136.9 %copy-start.8 = (f32[128,1120]{0,1:T(8,128)S(1)}, f32[128,1120]{0,1:T(8,128)}, u32[]{:S(2)}) copy-start(f32[128,1120]{0,1:T(8,128)} %copy-done.7) | copy-start | bytes 1720324
  326.9 136.9 %copy-start.67 = (f32[128]{0:T(128)S(1)}, f32[128]{0:T(128)}, u32[]{:S(2)}) copy-start(f32[128]{0:T(128)} %copy-done.66) | copy-start | bytes 1540
  326.9 136.9 %copy-start.69 = (f32[128]{0:T(128)S(1)}, f32[128]{0:T(128)}, u32[]{:S(2)}) copy-start(f32[128]{0:T(128)} %copy-done.68) | copy-start | bytes 1540
  326.9 136.9 %copy-start.75 = (f32[128]{0:T(128)S(1)}, f32[128]{0:T(128)}, u32[]{:S(2)}) copy-start(f32[128]{0:T(128)} %copy-done.74) | copy-start | bytes 1540
  327.0 136.9 %copy-start.77 = (f32[128]{0:T(128)S(1)}, f32[128]{0:T(128)}, u32[]{:S(2)}) copy-start(f32[128]{0:T(128)} %copy-done.76) | copy-start | bytes 1540
  327.0 139.1 %copy-start.88 = (f32[128]{0:T(128)S(1)}, f32[128]{0:T(128)}, u32[]{:S(2)}) copy-start(f32[128]{0:T(128)} %copy-done.87) | copy-start | bytes 1540
  327.0 139.1 %copy-start.90 = (f32[128]{0:T(128)S(1)}, f32[128]{0:T(128)}, u32[]{:S(2)}) copy-start(f32[128]{0:T(128)} %copy-done.89) | copy-start | bytes 1540
  327.0 174.1 %all-gather.19.cloned.1.call-start = ((), (), s32[]{:S(2)}) async-start(), calls=%async_computation.16 | async-start | bytes 1433600 | tf_op jit(solution)/shard_map/all_gather | solution.py:121
  468.2 5.0 copy-start.81
  468.2 5.0 copy-start.79
  470.0 64.0 %all-gather.23.cloned.1.call-start = ((), (), s32[]{:S(2)}) async-start(), calls=%async_computation.19 | async-start | bytes 1433600 | tf_op jit(solution)/shard_map/all_gather | solution.py:121
  473.3 27.8 %copy-start.21 = (bf16[280,1120]{1,0:T(8,128)(2,1)S(1)}, bf16[280,1120]{1,0:T(8,128)(2,1)}, u32[]{:S(2)}) copy-start(bf16[280,1120]{1,0:T(8,128)(2,1)} %param.16) | copy-start | bytes 1881604
  477.4 25.6 %copy-start.49 = (bf16[1,512,280]{1,2,0:T(8,128)(2,1)S(1)}, bf16[1,512,280]{1,2,0:T(8,128)(2,1)}, u32[]{:S(2)}) copy-start(bf16[1,512,280]{1,2,0:T(8,128)(2,1)} %copy-done.48) | copy-start | bytes 860164
  477.4 90.5 %reduce-scatter.29.cloned.1.call-start = ((), (), s32[]{:S(2)}) async-start(), calls=%async_computation.22 | async-start | bytes 1474560
  503.0 4.0 slice-start.3
  516.4 19.4 %copy-start.47 = (bf16[1,512,280]{1,2,0:T(8,128)(2,1)S(1)}, bf16[1,512,280]{1,2,0:T(8,128)(2,1)}, u32[]{:S(2)}) copy-start(bf16[1,512,280]{1,2,0:T(8,128)(2,1)} %copy-done.46) | copy-start | bytes 860164
  516.5 75.9 %reduce-scatter.31.cloned.1.call-start = ((), (), s32[]{:S(2)}) async-start(), calls=%async_computation.23 | async-start | bytes 1474560
  535.8 4.2 slice-start.1
  549.4 4.6 copy-start.38
  549.4 253.5 %all-reduce.4.cloned.1.call-start = ((), (), s32[]{:S(2)}) async-start(), calls=%async_computation.24 | async-start | bytes 30965760 | tf_op jit(solution)/shard_map/psum | solution.py:172
  549.8 4.2 copy-start.23
  554.0 4.2 copy-start.36
  554.0 4.2 copy-start.40
  566.0 27.5 %copy-start.57 = (f32[1120]{0:T(1024)S(1)}, f32[1120]{0:T(1024)}, u32[]{:S(2)}) copy-start(f32[1120]{0:T(1024)} %param.13) | copy-start | bytes 13444
  566.0 28.1 %copy-start.86 = (f32[128]{0:T(128)S(1)}, f32[128]{0:T(128)}, u32[]{:S(2)}) copy-start(f32[128]{0:T(128)} %copy-done.85) | copy-start | bytes 1540
  566.1 28.1 %copy-start.84 = (f32[128]{0:T(128)S(1)}, f32[128]{0:T(128)}, u32[]{:S(2)}) copy-start(f32[128]{0:T(128)} %copy-done.83) | copy-start | bytes 1540
  566.1 28.1 %copy-start.71 = (f32[128]{0:T(128)S(1)}, f32[128]{0:T(128)}, u32[]{:S(2)}) copy-start(f32[128]{0:T(128)} %copy-done.70) | copy-start | bytes 1540
  566.1 28.1 %copy-start.73 = (f32[128]{0:T(128)S(1)}, f32[128]{0:T(128)}, u32[]{:S(2)}) copy-start(f32[128]{0:T(128)} %copy-done.72) | copy-start | bytes 1540
  567.0 68.7 %copy-start.12 = (f32[128,1120]{0,1:T(8,128)S(1)}, f32[128,1120]{0,1:T(8,128)}, u32[]{:S(2)}) copy-start(f32[128,1120]{0,1:T(8,128)} %copy-done.11) | copy-start | bytes 1720324
  567.0 68.7 %copy-start.65 = (f32[128]{0:T(128)S(1)}, f32[128]{0:T(128)}, u32[]{:S(2)}) copy-start(f32[128]{0:T(128)} %copy-done.63) | copy-start | bytes 1540
  567.1 68.7 %copy-start.82 = (f32[128]{0:T(128)S(1)}, f32[128]{0:T(128)}, u32[]{:S(2)}) copy-start(f32[128]{0:T(128)} %copy-done.81) | copy-start | bytes 1540
  593.6 42.5 %copy-start.62 = (f32[128]{0:T(128)S(1)}, f32[128]{0:T(128)}, u32[]{:S(2)}) copy-start(f32[128]{0:T(128)} %copy-done.60) | copy-start | bytes 1540
  593.6 42.5 %copy-start.80 = (f32[128]{0:T(128)S(1)}, f32[128]{0:T(128)}, u32[]{:S(2)}) copy-start(f32[128]{0:T(128)} %copy-done.79) | copy-start | bytes 1540
  803.0 4.4 copy-start.26
  803.0 5.5 copy-start.9
  807.4 4.3 slice-start.4
  (57 other events, 102.9 us)
Sparse Core Ops, SparseCore 0:
  12.7 34.1 all-gather.8
  49.1 29.7 all-gather.12
  81.8 45.3 reduce-scatter.16
  130.1 46.4 reduce-scatter.18
  178.5 30.9 all-gather.20
  211.5 29.7 all-gather.14
  243.5 29.7 all-gather.16
  275.4 29.7 all-gather.10
  307.6 27.4 reduce-scatter.26
  337.9 27.8 reduce-scatter.24
  368.7 45.7 reduce-scatter.20
  417.3 46.4 reduce-scatter.22
  470.2 30.9 all-gather.18
  503.1 30.8 all-gather.22
  536.2 26.0 reduce-scatter.28
  564.5 27.8 reduce-scatter.30
  597.5 205.4 all-reduce.3
where the time goes:
time: 832 us; the launch traced here: 823 us
  waiting for transfers between devices  591 us (71%)
  matrix products  94.6 us (11%)
  blocking collectives  53.4 us (6%)
  local copies, waits for them, and re-layouts  41.6 us (5%)
  other arithmetic  24.5 us (3%)
  between operations  15.7 us (2%)
    psum x1, waiting for transfers between devices, shards(): lax.psum((grad_qkv, grad_out_weight, grad_up, grad_down), 'dp')  165 us
    reduce_scatter x2, waiting for transfers between devices, shards(): lax.psum_scatter(jnp.einsum('tf,df->td', up_grad_in, up_weight, preferred...  96.2 us
    reduce_scatter x2, waiting for transfers between devices, shards(): lax.psum_scatter(jnp.dot(heads_out, out_weight, preferred_element_type=jn...  84.2 us
    unnamed x21, waiting for transfers between devices  63.2 us
    all_gather x2, waiting for transfers between devices, shards(): gathered_two = lax.all_gather(norm_two, 'tensor', axis=0, tiled=True)  53.6 us
    all_gather x2, waiting for transfers between devices, shards(): lax.all_gather(grad_final.astype(jnp.bfloat16), 'tensor', axis=0, tiled=T...  46.5 us
    unnamed x220, local copies, waits for them, and re-layouts  41.5 us
    all_gather x2, waiting for transfers between devices, shards(): gathered_one = lax.all_gather(norm_one, 'tensor', axis=0, tiled=True)  41.1 us
  transfers between devices with their start and end apart: 17, of which 16 were waited for; matrix products, arithmetic and copies ran while one was open for 15% of the time, Pallas kernels for 0%

commit v1 on v0

v1 whole, which is shorter than its diff:
```python
import functools

import jax
import jax.numpy as jnp
from jax import lax
from jax.experimental import pallas as pl
from jax.experimental.pallas import tpu as pltpu
from jax.sharding import PartitionSpec as P


HD = 56
BF = jnp.bfloat16
F32 = jnp.float32
MESH = pl.DeviceIdType.MESH
NN = (((1,), (0,)), ((), ()))
NT = (((1,), (1,)), ((), ()))
TN = (((0,), (0,)), ((), ()))
COLS = 4
BITS = (1, 2)
NSEM = 256


def up_to(n, m):
    return -(-n // m) * m


def chunk_rows(rows):
    return up_to(-(-rows // COLS), 16)


def streams(ch):
    first = up_to(ch // 2, 16)
    return ((0, first, BITS, 0), (first, ch - first, BITS[::-1], 1))


def dg(a, b, dims):
    return lax.dot_general(a, b, dims, preferred_element_type=F32)


def normed(v):
    center = v - jnp.mean(v, axis=-1, keepdims=True)
    rstd = lax.rsqrt(jnp.mean(center * center, axis=-1, keepdims=True) + 1e-05)
    return center * rstd, rstd


def kernel(
    x_hbm, seg_ref, n1g, n1b, wq_hbm, wo_hbm, n2g, n2b, wu_hbm, wd_hbm, c_hbm,
    out_hbm, ig_hbm, gq_hbm, go_hbm, gu_hbm, gd_hbm, ng_ref,
    WQ, WO, WU, WD, GU, GD, RQ, RO, RU, RD, SQ, SO, SU, SD, KQ, KO, KU, KD,
    XS, CS, LAB, LT, BIAS, A1, QKV, PB0, PB1, O, HS, A2, Z, GP, GB, DHB, DO, DH, U,
    T2, S1, S2, SZ, R1, R2, RZ, OB, NG, NR,
    ssem, rsem, lsem,
):
    d = lax.axis_index("dp")
    z = lax.axis_index("tensor")
    c = lax.rem(d, 2)
    q = lax.rem(d // 2, COLS)
    zl = lax.rem(z, 2)
    zh = z // 2
    b = zl + 2 * c
    sw = zh != c
    dc = d + 1 - 2 * c
    z1 = z + 1 - 2 * zl
    z2 = z + 2 - 4 * zh
    core = (dc, z)
    zpeer = (d, z1)
    sigma = (dc, z2)

    def col(bit):
        on = lax.rem(q // bit, 2)
        return (d + 2 * bit * (1 - 2 * on), z)

    def flip(owner, bit):
        on = lax.rem(owner // bit, 2)
        return owner + bit * (1 - 2 * on)

    xpeer, ypeer = col(1), col(2)
    micro, tok, width = XS.shape
    row = 4 * tok
    heads = O.shape[1] // HD
    scale = HD ** (-0.5)
    counts = dict(r=0, l=0)
    pending = []

    def rcopy(src, dst, peer):
        i = counts["r"]
        counts["r"] = i + 1
        assert i < NSEM
        return pltpu.make_async_remote_copy(
            src_ref=src, dst_ref=dst, send_sem=ssem.at[i], recv_sem=rsem.at[i], device_id=peer, device_id_type=MESH
        )

    def lcopy(src, dst):
        i = counts["l"]
        counts["l"] = i + 1
        return pltpu.make_async_copy(src, dst, lsem.at[i])

    def rows(start, size, step=16):
        return pl.ds(pl.multiple_of(start, step), size)

    def blk(m, j):
        return pl.ds(pl.multiple_of(m * row + j * tok, tok), tok)

    def swapped(f):
        pl.when(sw)(f)

    def kept(f):
        pl.when(jnp.logical_not(sw))(f)

    barrier = pltpu.get_barrier_semaphore()
    peers = (core, zpeer, sigma, xpeer, ypeer)
    for p in peers:
        pl.semaphore_signal(barrier, 1, device_id=p, device_id_type=MESH)
    pl.semaphore_wait(barrier, len(peers))

    class Gather:
        def __init__(self, view):
            self.view = view
            self.cz = rcopy(view(b), view(b), zpeer)
            self.cc = rcopy(view(b), view(b), core)
            far = 1 - zl + 2 * c
            self.cf = rcopy(view(far), view(far), core)

        def start(self):
            self.cz.start()
            self.cc.start()

        def forward(self):
            self.cz.wait_recv()
            self.cf.start()

        def finish(self):
            self.cc.wait_recv()
            self.cf.wait_recv()
            pending.extend([self.cz, self.cc, self.cf])

    def gather_rows(ref, m):
        return Gather(lambda j: ref.at[blk(m, j)])

    class Scatter:
        def __init__(self, s):
            self.s = s
            self.c1 = rcopy(S1.at[s], R1.at[s], core)
            self.c2 = rcopy(S2.at[s], R2.at[s], core)
            self.cz = rcopy(SZ.at[s], RZ.at[s], zpeer)

        def start(self, term):
            s = self.s
            away = 1 - zl
            part = term(away + 2 * (1 - c), away + 2 * c)
            S1[s] = part[:tok].astype(BF)
            self.c1.start()
            keep = part[tok:]
            part = term(zl + 2 * (1 - c), zl + 2 * c)
            S2[s] = part[:tok].astype(BF)
            T2[s] = part[tok:]
            self.c2.start()
            self.c1.wait_recv()
            SZ[s] = (keep + R1[s].astype(F32)).astype(BF)
            self.cz.start()

        def finish(self):
            s = self.s
            self.c2.wait_recv()
            self.cz.wait_recv()
            total = T2[s] + R2[s].astype(F32) + RZ[s].astype(F32)
            for cp in (self.c1, self.c2, self.cz):
                cp.wait_send()
            return total

    class Weight:
        def __init__(self, hbm, ref):
            self.hbm, self.ref = hbm, ref
            have, total = hbm.shape[0], ref.shape[0]
            self.ch = ch = total // COLS
            self.local = lcopy(hbm, ref.at[0:have])
            self.hops = []
            for off, size, order, _ in streams(ch):
                i = counts["r"]
                counts["r"] = i + 1
                first = []
                for short in (False, True):
                    lost = max(0, total - have)
                    n = size - min(lost, size) if short and off else size
                    at = rows(q * ch + off, n)
                    cp = pltpu.make_async_remote_copy(
                        src_ref=hbm.at[at], dst_ref=ref.at[at], send_sem=ssem.at[i], recv_sem=rsem.at[i],
                        device_id=sigma, device_id_type=MESH,
                    )
                    first.append((n, cp))
                steps, done = [], [0]
                for bit in order:
                    copies = []
                    for s in done:
                        owner = q
                        for k in BITS:
                            if s & k:
                                owner = flip(owner, k)
                        at = rows(owner * ch + off, size)
                        copies.append(rcopy(ref.at[at], ref.at[at], col(bit)))
                    steps.append(copies)
                    done = done + [s | bit for s in done]
                self.hops.append((size, first, steps))

        def each_first(self, act):
            for size, ((_, whole), (n, part)) in [(h[0], h[1]) for h in self.hops]:
                if n == size:
                    act(whole)
                else:
                    pl.when(q < COLS - 1)(functools.partial(act, whole))
                    pl.when(q == COLS - 1)(functools.partial(act, part))

        def send(self):
            swapped(lambda: self.each_first(lambda cp: cp.start()))

        def load(self):
            kept(self.local.start)

        def stage(self, j):
            def go():
                if j == 0:
                    self.each_first(lambda cp: cp.wait_recv())
                else:
                    for _, _, steps in self.hops:
                        for cp in steps[j - 1]:
                            cp.wait_recv()
                for _, _, steps in self.hops:
                    for cp in steps[j]:
                        cp.start()

            swapped(go)

        def finish(self):
            def go():
                for _, _, steps in self.hops:
                    for cp in steps[-1]:
                        cp.wait_recv()
                self.each_first(lambda cp: cp.wait_send())
                for _, _, steps in self.hops:
                    for copies in steps:
                        for cp in copies:
                            cp.wait_send()

            swapped(go)
            kept(self.local.wait)

    class Grad:
        def __init__(self, ref, lanes, recv, far, near, hbm):
            self.ref, self.lanes, self.recv, self.far, self.near, self.hbm = ref, lanes, recv, far, near, hbm
            self.ch = ch = recv.shape[1]
            self.parts = []
            for off, size, order, fin in streams(ch):
                part = dict(off=off, size=size, order=order, fin=fin)
                base, steps = 0, []
                for j, bit in enumerate(order):
                    rest = [0]
                    for k in order[j + 1 :]:
                        rest = rest + [s | k for s in rest]
                    copies = []
                    for i, s in enumerate(rest):
                        mine = q
                        for k in BITS:
                            if s & k:
                                mine = flip(mine, k)
                        theirs = flip(mine, bit)
                        slot = recv.at[base + i, off : off + size]
                        copies.append((mine, base + i, rcopy(self.at(theirs, off, size), slot, col(bit))))
                    base += len(rest)
                    steps.append(copies)
                part["rs"] = steps
                part["sigma"] = rcopy(self.at(q, off, size), far.at[off : off + size], sigma)
                part["near"] = rcopy(self.at(q, off, size), near.at[0:size], core)
                part["own"] = lcopy(self.at(q, off, size), self.out(q, off, size))
                part["own_core"] = rcopy(self.at(q, off, size), self.out(q, off, size), core)
                done, spread = [0], []
                for bit in order:
                    copies = []
                    for s in done:
                        owner = q
                        for k in BITS:
                            if s & k:
                                owner = flip(owner, k)
                        src = self.at(q, off, size) if s == 0 else self.out(owner, off, size)
                        got = flip(owner, bit)
                        copies.append(
                            (
                                rcopy(src, self.out(owner, off, size), col(bit)),
                                rcopy(self.out(got, off, size), self.out(got, off, size), core),
                            )
                        )
                    spread.append(copies)
                    done = done + [s | bit for s in done]
                part["spread"] = spread
                self.parts.append(part)

        def at(self, owner, off, size):
            return self.ref.at[rows(owner * self.ch + off, size), 0 : self.lanes]

        def out(self, owner, off, size):
            return self.hbm.at[rows(owner * self.ch + off, size)]

        def reduce_send(self, j):
            for p in self.parts:
                for _, _, cp in p["rs"][j]:
                    cp.start()

        def reduce_add(self, j):
            for p in self.parts:
                off, size = p["off"], p["size"]
                for mine, slot, cp in p["rs"][j]:
                    cp.wait_recv()
                    r = rows(mine * self.ch + off, size)
                    total = self.ref[r, 0 : self.lanes].astype(F32) + self.recv[slot, off : off + size].astype(F32)
                    self.ref[r, 0 : self.lanes] = total.astype(BF)
                    pending.append(cp)

        def sigma_send(self):
            swapped(lambda: [p["sigma"].start() for p in self.parts] and None)

        def sigma_take(self):
            def go():
                for p in self.parts:
                    off, size = p["off"], p["size"]
                    p["sigma"].wait()
                    self.ref[rows(q * self.ch + off, size), 0 : self.lanes] = self.far[off : off + size]

            swapped(go)

        def near_send(self):
            for p in self.parts:
                pl.when(c != p["fin"])(p["near"].start)

        def near_add(self):
            for p in self.parts:

                def give(p=p):
                    p["near"].wait_send()

                def take(p=p):
                    p["near"].wait_recv()
                    r = rows(q * self.ch + p["off"], p["size"])
                    total = self.ref[r, 0 : self.lanes].astype(F32) + self.near[0 : p["size"]].astype(F32)
                    self.ref[r, 0 : self.lanes] = total.astype(BF)
                    for cp, _ in p["spread"][0]:
                        cp.start()
                    p["own_core"].start()
                    p["own"].start()

                pl.when(c != p["fin"])(give)
                pl.when(c == p["fin"])(take)

        def spread(self, j):
            for p in self.parts:

                def go(p=p):
                    for cp, _ in p["spread"][j]:
                        cp.wait_recv()
                    if j + 1 < len(p["spread"]):
                        for cp, _ in p["spread"][j + 1]:
                            cp.start()
                    for _, cp in p["spread"][j]:
                        cp.start()

                pl.when(c == p["fin"])(go)

        def finish(self):
            for p in self.parts:

                def owner(p=p):
                    p["own"].wait()
                    p["own_core"].wait_send()
                    for copies in p["spread"]:
                        for a, f in copies:
                            a.wait_send()
                            f.wait_send()

                def other(p=p):
                    p["own_core"].wait_recv()
                    for copies in p["spread"]:
                        for _, f in copies:
                            f.wait_recv()

                pl.when(c == p["fin"])(owner)
                pl.when(c != p["fin"])(other)

    wq, wo, wu, wd = Weight(wq_hbm, WQ), Weight(wo_hbm, WO), Weight(wu_hbm, WU), Weight(wd_hbm, WD)
    other_b = zl + 2 * (1 - c)
    x_swap = [rcopy(x_hbm.at[m], XS.at[m], sigma) for m in range(micro)]
    x_load = [lcopy(x_hbm.at[m], XS.at[m]) for m in range(micro)]
    c_swap = rcopy(c_hbm, CS, sigma)
    c_load = lcopy(c_hbm, CS)
    lab_swap = rcopy(seg_ref, LAB.at[other_b], sigma)
    lab_gather = Gather(lambda j: LAB.at[j])
    a1_gather = [gather_rows(A1, m) for m in range(micro)]
    gb_gather = [gather_rows(GB, m) for m in range(micro)]
    a2_gather = [gather_rows(A2, m) for m in range(micro)]
    dhb_gather = [gather_rows(DHB, m) for m in range(micro)]

    def first_norm(m):
        swapped(x_swap[m].wait_recv)
        kept(x_load[m].wait)
        xhat, _ = normed(XS[m].astype(F32))
        A1[blk(m, b), :] = (xhat * n1g[...] + n1b[...]).astype(BF)
        a1_gather[m].start()

    def labels_wide():
        for m in range(micro):
            for j in range(4):
                lab = LAB[j, m : m + 1, :].astype(F32)
                LT[m, j * tok : (j + 1) * tok, :] = jnp.transpose(jnp.broadcast_to(lab, (tok, tok)))

    def loss_grad():
        swapped(c_swap.wait_recv)
        kept(c_load.wait)
        for m in range(micro):
            live = (LT[m, pl.ds(pl.multiple_of(b * tok, tok), tok), 0:1] >= 0.0).astype(F32)
            GB[blk(m, b), :] = (CS[m].astype(F32) * live).astype(BF)
            gb_gather[m].start()

    def make_bias(m):
        for j in range(4):
            lab = LAB[j, m : m + 1, :].astype(F32)
            place_q = lax.broadcasted_iota(jnp.int32, (row, tok), 0)
            place_k = lax.broadcasted_iota(jnp.int32, (row, tok), 1) + j * tok
            ok = (LT[m] == lab) & (place_k <= place_q)
            BIAS[:, j * tok : (j + 1) * tok] = jnp.where(ok, 0.0, -1e30)

    half = row // 2
    local_width = O.shape[1]

    def qkv_slices(m, h, qb):
        nk = (qb + 1) * half
        at = m * row
        q0 = at + qb * half
        e0, e1, e2 = h * HD, local_width + h * HD, 2 * local_width + h * HD
        return (
            slice(q0, q0 + half),
            slice(at, at + nk),
            slice(e0, e0 + HD),
            slice(e1, e1 + HD),
            slice(e2, e2 + HD),
        )

    def project(m):
        at = slice(m * row, (m + 1) * row)
        QKV[at, :] = dg(A1[at, :], WQ[0:width, :], NN).astype(BF)

    def attend(m):
        for h in range(heads):
            for qb, PB in ((0, PB0), (1, PB1)):
                rq, rk, eq, ek, ev = qkv_slices(m, h, qb)
                s = dg(QKV[rq, eq], QKV[rk, ek], NT) * scale
                s = s + BIAS[qb * half : (qb + 1) * half, 0 : (qb + 1) * half]
                e = jnp.exp(s - jnp.max(s, axis=-1, keepdims=True))
                p = (e * (1.0 / jnp.sum(e, axis=-1, keepdims=True))).astype(BF)
                PB[m, h] = p
                O[rq, eq] = dg(p, QKV[rk, ev], NN).astype(BF)

    def attend_back(m):
        for h in range(heads):
            for qb, PB in ((1, PB1), (0, PB0)):
                rq, rk, eq, ek, ev = qkv_slices(m, h, qb)
                qv, do, pb = QKV[rq, eq], DO[rq, eq], PB[m, h]
                kv = QKV[rk, ek]
                dp = dg(do, QKV[rk, ev], NT)
                p = pb.astype(F32)
                pdp = p * dp
                ds = (pdp - p * jnp.sum(pdp, axis=-1, keepdims=True)).astype(BF)
                dq = (dg(ds, kv, NN) * scale).astype(BF)
                dk, dv = dg(ds, qv, TN), dg(pb, do, TN)
                if qb == 1:
                    dq1, dk1, dv1, rq1 = dq, dk, dv, rq
                else:
                    QKV[rq, eq] = dq
                    QKV[rq1, eq] = dq1
                    QKV[rq, ek] = ((dk1[:half] + dk) * scale).astype(BF)
                    QKV[rq1, ek] = (dk1[half:] * scale).astype(BF)
                    QKV[rq, ev] = (dv1[:half] + dv).astype(BF)
                    QKV[rq1, ev] = dv1[half:].astype(BF)

    def pair(ref, m, i, j):
        return jnp.concatenate([ref[blk(m, i), :], ref[blk(m, j), :]], axis=0)

    def second_norm(m, total):
        h = XS[m].astype(F32) + total
        HS[m] = h
        xhat, _ = normed(h)
        A2[blk(m, b), :] = (xhat * n2g[...] + n2b[...]).astype(BF)
        a2_gather[m].start()

    def up(m):
        for part in range(2):
            up_half(m * row + part * half)

    def up_half(at):
        U[...] = dg(A2[at : at + half, :], WU[0:width, :], NN)
        c0 = 0.7978845608028654
        step = 32

        def body(i, carry):
            r = rows(i * step, step, step)
            w = rows(at + i * step, step, step)
            u = U[r, :]
            u2 = u * u
            t = jnp.tanh(c0 * u * (1.0 + 0.044715 * u2))
            hp = 0.5 * (1.0 + t)
            Z[w, :] = (u * hp).astype(BF)
            GP[w, :] = (hp + (0.5 * c0) * u * (1.0 - t * t) * (1.0 + (3 * 0.044715) * u2)).astype(BF)
            return carry

        lax.fori_loop(0, half // step, body, 0)

    def down_back(m):
        at = slice(m * row, (m + 1) * row)
        dz = dg(GB[at, :], WD[0 : Z.shape[1], :], NT)
        GP[at, :] = (dz * GP[at, :].astype(F32)).astype(BF)

    def norm_back(v, gain, grad):
        xhat, rstd = normed(v)
        gains = jnp.sum(grad * xhat, axis=0, keepdims=True)
        shifts = jnp.sum(grad, axis=0, keepdims=True)
        dn = grad * gain
        dv = rstd * (
            dn - jnp.mean(dn, axis=-1, keepdims=True) - xhat * jnp.mean(dn * xhat, axis=-1, keepdims=True)
        )
        return dv, gains, shifts

    def second_norm_back(m, total):
        dv, gains, shifts = norm_back(HS[m], n2g[...], total)
        NG[2:3, :] += gains
        NG[3:4, :] += shifts
        dh = GB[blk(m, b), :].astype(F32) + dv
        DH[m] = dh
        DHB[blk(m, b), :] = dh.astype(BF)
        dhb_gather[m].start()

    def first_norm_back(m, total):
        dv, gains, shifts = norm_back(XS[m].astype(F32), n1g[...], total)
        NG[0:1, :] += gains
        NG[1:2, :] += shifts
        return DH[m] + dv

    NG[...] = jnp.zeros_like(NG)
    wq.send()
    swapped(lambda: (lab_swap.start(), x_swap[0].start(), x_swap[1].start()) and None)
    kept(lambda: (x_load[0].start(), x_load[1].start(), c_load.start()) and None)
    for w in (wq, wo, wu, wd):
        w.load()

    @pl.when(jnp.logical_not(sw))
    def _():
        LAB[b] = seg_ref[...]

    swapped(lab_swap.wait_recv)
    lab_gather.start()
    first_norm(0)
    wq.stage(0)
    first_norm(1)
    swapped(c_swap.start)
    wo.send()
    lab_gather.forward()
    a1_gather[0].forward()
    lab_gather.finish()
    labels_wide()
    make_bias(0)
    wq.stage(1)
    wu.send()
    a1_gather[1].forward()
    wo.stage(0)
    a1_gather[0].finish()
    wq.finish()

    attn_sum = [Scatter(2 * m) for m in range(micro)]
    mid_sum = [Scatter(2 * m) for m in range(micro)]
    y_sum = [Scatter(2 * m + 1) for m in range(micro)]
    in_sum = [Scatter(2 * m) for m in range(micro)]

    def out_term(m):
        return lambda i, j: dg(pair(O, m, i, j), WO[0:local_width, :], NN)

    def y_term(m):
        return lambda i, j: dg(pair(Z, m, i, j), WD[0 : Z.shape[1], :], NN)

    def mid_term(m):
        return lambda i, j: dg(pair(GP, m, i, j), WU[0:width, :], NT)

    def in_term(m):
        return lambda i, j: dg(pair(QKV, m, i, j), WQ[0:width, :], NT)

    project(0)
    loss_grad()
    wo.stage(1)
    wd.send()
    attend(0)
    wu.stage(0)
    wo.finish()
    attn_sum[0].start(out_term(0))
    for m in range(micro):
        gb_gather[m].forward()
    a1_gather[1].finish()
    make_bias(1)
    project(1)
    wu.stage(1)
    attend(1)
    wd.stage(0)
    attn_sum[1].start(out_term(1))
    second_norm(0, attn_sum[0].finish())
    wd.stage(1)
    second_norm(1, attn_sum[1].finish())
    a2_gather[0].forward()
    wu.finish()
    a2_gather[0].finish()
    up(0)
    a2_gather[1].forward()
    wd.finish()
    gb_gather[0].finish()
    down_back(0)
    mid_sum[0].start(mid_term(0))
    a2_gather[1].finish()
    up(1)
    gb_gather[1].finish()
    down_back(1)
    mid_sum[1].start(mid_term(1))
    second_norm_back(0, mid_sum[0].finish())
    y_sum[0].start(y_term(0))
    second_norm_back(1, mid_sum[1].finish())
    y_sum[1].start(y_term(1))
    dhb_gather[0].forward()

    gq = Grad(WU, gq_hbm.shape[1], RQ, SQ, KQ, gq_hbm)
    go = Grad(WD, width, RO, SO, KO, go_hbm)
    gu = Grad(GU, gu_hbm.shape[1], RU, SU, KU, gu_hbm)
    gd = Grad(GD, width, RD, SD, KD, gd_hbm)
    ff = Z.shape[1]
    GD[0:ff, :] = dg(Z[...], GB[...], TN).astype(BF)
    GD[ff:, :] = jnp.zeros((GD.shape[0] - ff, width), BF)
    gd.reduce_send(0)
    dhb_gather[1].forward()
    GU[0:width, :] = dg(A2[...], GP[...], TN).astype(BF)
    GU[width:, :] = jnp.zeros((GU.shape[0] - width, ff), BF)
    dhb_gather[0].finish()

    def heads_back(m):
        at = slice(m * row, (m + 1) * row)
        DO[at, :] = dg(DHB[at, :], WO[0:local_width, :], NT).astype(BF)
        attend_back(m)

    heads_back(0)
    gd.reduce_add(0)
    gd.reduce_send(1)
    gu.reduce_send(0)
    in_sum[0].start(in_term(0))
    dhb_gather[1].finish()
    WD[0:local_width, :] = dg(O[...], DHB[...], TN).astype(BF)
    gd.reduce_add(1)
    gd.sigma_send()
    heads_back(1)
    gu.reduce_add(0)
    gu.reduce_send(1)
    in_sum[1].start(in_term(1))
    WU[0:width, 0 : 3 * local_width] = dg(A1[...], QKV[...], TN).astype(BF)
    gq.reduce_send(0)
    go.reduce_send(0)
    gd.sigma_take()
    gd.near_send()
    gu.reduce_add(1)
    gu.sigma_send()
    gd.near_add()

    out_swap = [rcopy(OB.at[m], out_hbm.at[m], sigma) for m in range(micro)]
    out_keep = [lcopy(OB.at[m], out_hbm.at[m]) for m in range(micro)]
    ig_swap = [rcopy(XS.at[m], CS.at[m], sigma) for m in range(micro)]
    ig_keep = [lcopy(DH.at[m], ig_hbm.at[m]) for m in range(micro)]
    for m in range(micro):
        OB[m] = (HS[m] + y_sum[m].finish()).astype(BF)
        swapped(out_swap[m].start)
        kept(out_keep[m].start)
    gq.reduce_add(0)
    gq.reduce_send(1)
    go.reduce_add(0)
    go.reduce_send(1)
    gu.sigma_take()
    gu.near_send()
    for m in range(micro):
        dx = first_norm_back(m, in_sum[m].finish())
        DH[m] = dx

        @pl.when(sw)
        def _():
            XS[m] = dx.astype(BF)
            ig_swap[m].start()

        kept(ig_keep[m].start)
    gu.near_add()
    gd.spread(0)
    gq.reduce_add(1)
    gq.sigma_send()
    go.reduce_add(1)
    go.sigma_send()
    sums = iter([rcopy(NG, NR.at[i], p) for i, p in enumerate((core, zpeer, sigma, xpeer, ypeer))])

    def sum_send():
        cp = next(sums)
        cp.start()
        return cp

    def sum_add(i, cp):
        cp.wait()
        NG[...] = NG[...] + NR[i]

    cp = sum_send()
    gu.spread(0)
    gd.spread(1)
    sum_add(0, cp)
    cp = sum_send()
    gu.spread(1)
    sum_add(1, cp)
    cp = sum_send()
    gq.sigma_take()
    gq.near_send()
    go.sigma_take()
    go.near_send()
    gq.near_add()
    go.near_add()
    sum_add(2, cp)
    cp = sum_send()
    gq.spread(0)
    go.spread(0)
    sum_add(3, cp)
    cp = sum_send()
    gq.spread(1)
    go.spread(1)
    sum_add(4, cp)
    ng_ref[...] = NG[...]
    for m in range(micro):

        @pl.when(sw)
        def _():
            ig_swap[m].wait()
            DH[m] = CS[m].astype(F32)
            ig_keep[m].start()
            out_swap[m].wait()
            c_in = x_swap[m]
            c_in.wait_send()

        ig_keep[m].wait()
        kept(out_keep[m].wait)
    swapped(lambda: (c_swap.wait_send(), lab_swap.wait_send()) and None)
    lab_gather_sends = []
    for cp in pending + lab_gather_sends:
        cp.wait_send()
    for g in (gd, gu, gq, go):
        g.finish()


def layer(
    inputs, segments, norm1_gain, norm1_bias, qkv_weight, out_weight, norm2_gain, norm2_bias, up_weight, down_weight,
    cotangent,
):
    micro, tok, width = inputs.shape
    local_width = qkv_weight.shape[2]
    ff = up_weight.shape[1]
    row = 4 * tok
    heads = local_width // HD
    three = 3 * local_width
    wide = up_to(three, 128)
    half = row // 2
    cq, co, cu, cd = chunk_rows(width), chunk_rows(local_width), chunk_rows(width), chunk_rows(ff)
    wq = jnp.transpose(qkv_weight, (1, 0, 2)).reshape(width, three)
    wq = jnp.pad(wq, ((0, COLS * cq - width), (0, 0)))
    wo = jnp.pad(out_weight, ((0, COLS * co - local_width), (0, 0)))

    def v(shape, dtype=BF):
        return pltpu.VMEM(shape, dtype)

    def recv(ch, lanes):
        return v((COLS - 1, ch, lanes))

    def near(ch, lanes):
        return v((max(size for _, size, _, _ in streams(ch)), lanes))

    any_spec = pl.BlockSpec(memory_space=pl.ANY)
    vmem = pl.BlockSpec(memory_space=pltpu.VMEM)
    scratch = [
        v((COLS * cq, three)), v((COLS * co, width)), v((COLS * cu, ff)), v((COLS * cd, width)),
        v((COLS * cu, ff)), v((COLS * cd, width)),
        recv(cq, wide), recv(co, width), recv(cu, ff), recv(cd, width),
        v((cq, wide)), v((co, width)), v((cu, ff)), v((cd, width)),
        near(cq, wide), near(co, width), near(cu, ff), near(cd, width),
        v((micro, tok, width)), v((micro, tok, width)), v((4, micro, tok), jnp.int32), v((micro, row, tok), F32),
        v((row, row), F32),
        v((micro * row, width)), v((micro * row, three)),
        v((micro, heads, half, half)), v((micro, heads, half, row)), v((micro * row, local_width)),
        v((micro, tok, width), F32),
        v((micro * row, width)), v((micro * row, ff)), v((micro * row, ff)), v((micro * row, width)),
        v((micro * row, width)), v((micro * row, local_width)), v((micro, tok, width), F32), v((half, ff), F32),
        v((2 * micro, tok, width), F32),
        v((2 * micro, tok, width)), v((2 * micro, tok, width)), v((2 * micro, tok, width)),
        v((2 * micro, tok, width)), v((2 * micro, tok, width)), v((2 * micro, tok, width)),
        v((micro, tok, width)),
        v((8, width), F32), v((5, 8, width), F32),
        pltpu.SemaphoreType.DMA((NSEM,)), pltpu.SemaphoreType.DMA((NSEM,)), pltpu.SemaphoreType.DMA((32,)),
    ]
    out, input_grad, gq, go, gu, gd, ng = pl.pallas_call(
        kernel,
        out_shape=[
            jax.ShapeDtypeStruct((micro, tok, width), BF),
            jax.ShapeDtypeStruct((micro, tok, width), F32),
            jax.ShapeDtypeStruct((COLS * cq, wide), BF),
            jax.ShapeDtypeStruct((COLS * co, width), BF),
            jax.ShapeDtypeStruct((COLS * cu, ff), BF),
            jax.ShapeDtypeStruct((COLS * cd, width), BF),
            jax.ShapeDtypeStruct((8, width), F32),
        ],
        in_specs=[any_spec, vmem, vmem, vmem, any_spec, any_spec, vmem, vmem, any_spec, any_spec, any_spec],
        out_specs=[any_spec] * 6 + [vmem],
        scratch_shapes=scratch,
        compiler_params=pltpu.CompilerParams(
            collective_id=0, has_side_effects=True, vmem_limit_bytes=64 * 1024 * 1024
        ),
    )(
        inputs, segments, norm1_gain[None], norm1_bias[None], wq, wo, norm2_gain[None], norm2_bias[None], up_weight,
        down_weight, cotangent,
    )
    grads = (
        jnp.transpose(gq[:width, :three].reshape(width, 3, local_width), (1, 0, 2)).astype(F32),
        go[:local_width].astype(F32),
        gu[:width].astype(F32),
        gd[:ff].astype(F32),
    )
    extent = lax.axis_size("dp")
    block = 2 * COLS
    if extent > block:
        groups = [[r + block * j for j in range(extent // block)] for r in range(block)]
        grads = lax.psum(grads, "dp", axis_index_groups=groups)
        ng = lax.psum(ng, "dp", axis_index_groups=groups)
    gq, go, gu, gd = grads
    return out, input_grad, ng[0], ng[1], gq, go, ng[2], ng[3], gu, gd


def solution(mesh):
    tokens = P(None, ("dp", "tensor"), None)
    weights = (P(None, None, "tensor"), P("tensor", None))
    mlp = (P(None, "tensor"), P("tensor", None))
    return jax.shard_map(
        layer,
        mesh=mesh,
        in_specs=(tokens, P(None, ("dp", "tensor")), P(), P(), *weights, P(), P(), *mlp, tokens),
        out_specs=(tokens, tokens, P(), P(), *weights, P(), P(), *mlp),
        check_vma=False,
    )
```

time: 832 us -> 300 us (0.36)
  waiting for transfers between devices: 591 us -> 0 us
  Pallas kernels: 0 us -> 266 us
  matrix products: 94.6 us -> 0 us
  blocking collectives: 53.4 us -> 0 us
  local copies, waits for them, and re-layouts: 41.6 us -> 19.3 us
  between operations: 15.7 us -> 0.99 us
  other arithmetic: 24.5 us -> 10.6 us
    pallas_call x0 -> x1, Pallas kernels: none -> 266 us  [layer(): pl.pallas_call(kernel, out_shape=[jax.ShapeDtypeStruct((micro, tok, width...]
    all_gather x8 -> x0, waiting for transfers between devices: 182 us -> none  [the longest x2 53.6 us: shards(): gathered_two = lax.all_gather(norm_two, 'tensor', axis=0, tiled=True)]
    reduce_scatter x4 -> x0, waiting for transfers between devices: 180 us -> none  [the longest x2 96.2 us: shards(): lax.psum_scatter(jnp.einsum('tf,df->td', up_grad_in, up_weight, preferred...]
    psum x1 -> x0, waiting for transfers between devices: 165 us -> none  [shards(): lax.psum((grad_qkv, grad_out_weight, grad_up, grad_down), 'dp')]
    dot_general x36 -> x0, matrix products: 94.6 us -> none  [the longest x2 12.3 us: shards(): jnp.dot(gathered_two, up_weight, preferred_element_type=jnp.float32)]
    unnamed x21 -> x0, waiting for transfers between devices: 63.2 us -> none
    psum x1 -> x0, blocking collectives: 40.8 us -> none  [shards(): lax.psum((gain_one, shift_one, gain_two, shift_two), ('dp', 'tensor'))]
    unnamed x220 -> x28, local copies, waits for them, and re-layouts: 41.5 us -> 5.23 us
  transfers between devices with their start and end apart: 17 -> 0, of which waited for: 16 -> 0; matrix products, arithmetic and copies ran while one was open for 15% -> 0% of each run, Pallas kernels for 0% -> 0%
where the time goes in v1:
time: 300 us; the launch traced here: 297 us
  Pallas kernels  266 us (89%)
  local copies, waits for them, and re-layouts  19.3 us (6%)
  other arithmetic  10.6 us (4%)
    pallas_call x1, Pallas kernels, layer(): pl.pallas_call(kernel, out_shape=[jax.ShapeDtypeStruct((micro, tok, width...  266 us
    convert_element_type x1, other arithmetic, layer(): gd[:ff].astype(F32)  7.35 us

profile of v1, /device:TPU:0, one launch (start us, length us, event | category | flops | bytes accessed | tf_op | source)
XLA Modules:
  0.0 297.0 jit_solution(7625159864707248209)
XLA Ops:
  0.6 3.1 %copy.33 = bf16[1120,840]{1,0:T(8,128)(2,1)S(1)} copy(bf16[1120,840]{0,1:T(8,128)(2,1)} %bitcast.7) | data formatting | bytes 3763200 | tf_op jit(solution)/shard_map/reshape | solution.py:769
  3.8 0.0 copy-start.2
  3.8 0.0 copy-start.4
  3.8 0.0 copy-start.5
  3.8 1.5 pad.8.wq_hbm
  5.3 0.0 copy-done.2
  5.3 0.0 copy-start.8
  5.3 0.0 copy-start.9
  5.3 0.0 copy-start.10
  5.3 0.0 copy-start.11
  5.3 0.9 pad.9.wo_hbm
  6.2 0.0 copy-done.4
  6.2 1.1 copy.34.x_hbm
  7.3 0.0 copy-done.5
  7.3 1.1 copy.35.c_hbm
  8.4 0.0 copy-done.8
  8.4 0.6 broadcast_in_dim.12.n1g
  9.0 0.0 copy-done.9
  9.0 0.6 broadcast_in_dim.13.n1b
  9.6 0.0 copy-done.10
  9.6 0.6 broadcast_in_dim.14.n2g
  10.2 0.0 copy-done.11
  10.2 0.6 broadcast_in_dim.15.n2b
  10.8 266.1 %shard_map.186 = (bf16[2,128,1120]{2,1,0:T(8,128)(2,1)}, f32[2,128,1120]{2,1,0:T(8,128)}, bf16[1152,896]{1,0:T(8,128)(2,1)}, bf16[320,1120]{1,0:T(8,128)(2,1)}, ...) custom-call(bf16[2,128,1120]{2,1,0:T(8,128)(2,1)} %copy.34.x_hbm, s32[2,128]{1,0:T(2,128)} %seg_ref.1, ...), custom_call_target="tpu_custom_call" | custom-call | tf_op jit(solution)/shard_map/pallas_call | solution.py:804
  276.9 0.0 copy-start.7
  276.9 0.0 copy-start
  276.9 7.3 %slice_convert_fusion = (f32[1120,1120]{1,0:T(8,128)}, f32[1120,1120]{1,0:T(8,128)}) fusion(bf16[1152,1120]{1,0:T(8,128)(2,1)} %get-tuple-element.23, bf16[1152,1120]{1,0:T(8,128)(2,1)} %get-tuple-element.22), kind=kLoop, calls=%fused_computation | loop fusion | flops 2508800 | bytes 15052800 | tf_op jit(solution)/shard_map/convert_element_type | solution.py:829
  284.3 0.0 copy-done.7
  284.3 0.7 slice_reduce_fusion
  284.9 0.0 copy-done
  284.9 2.1 slice_convert_fusion.2
  287.1 0.0 copy-start.6
  287.1 5.5 %copy.36 = f32[1120,840]{0,1:T(8,128)} copy(f32[1120,840]{1,0:T(8,128)} %slice_convert_fusion.2) | data formatting | bytes 7526400 | tf_op jit(solution)/shard_map/convert_element_type | solution.py:826
  292.6 0.0 copy-start.1
  292.6 0.0 copy-start.3
  292.6 0.0 copy-done.6
  292.6 1.1 slice_convert_fusion.3
  293.7 0.6 copy-done.1
  294.3 1.4 copy.38
  295.7 0.0 copy-done.3
  295.7 1.1 copy.37
Async XLA Ops:
  3.8 1.5 copy-start.2
  3.8 2.4 copy-start.4
  3.8 3.5 %copy-start.5 = (bf16[2,128,1120]{1,2,0:T(8,128)(2,1)S(1)}, bf16[2,128,1120]{1,2,0:T(8,128)(2,1)}, u32[]{:S(2)}) copy-start(bf16[2,128,1120]{1,2,0:T(8,128)(2,1)} %param.21) | copy-start | bytes 1720324
  5.3 3.1 %copy-start.8 = (f32[1120]{0:T(1024)S(1)}, f32[1120]{0:T(1024)}, u32[]{:S(2)}) copy-start(f32[1120]{0:T(1024)} %param.13) | copy-start | bytes 13444
  5.3 3.7 %copy-start.9 = (f32[1120]{0:T(1024)S(1)}, f32[1120]{0:T(1024)}, u32[]{:S(2)}) copy-start(f32[1120]{0:T(1024)} %param.14) | copy-start | bytes 13444
  5.3 4.3 %copy-start.10 = (f32[1120]{0:T(1024)S(1)}, f32[1120]{0:T(1024)}, u32[]{:S(2)}) copy-start(f32[1120]{0:T(1024)} %param.17) | copy-start | bytes 13444
  5.3 4.9 %copy-start.11 = (f32[1120]{0:T(1024)S(1)}, f32[1120]{0:T(1024)}, u32[]{:S(2)}) copy-start(f32[1120]{0:T(1024)} %param.18) | copy-start | bytes 13444
  276.9 7.4 %copy-start.7 = (f32[8,1120]{1,0:T(8,128)S(1)}, f32[8,1120]{1,0:T(8,128)}, u32[]{:S(2)}) copy-start(f32[8,1120]{1,0:T(8,128)} %get-tuple-element.19) | copy-start | bytes 107524
  276.9 8.0 %copy-start = (bf16[1152,896]{1,0:T(8,128)(2,1)S(1)}, bf16[1152,896]{1,0:T(8,128)(2,1)}, u32[]{:S(2)}) copy-start(bf16[1152,896]{1,0:T(8,128)(2,1)} %get-tuple-element.20) | copy-start | bytes 6193156
  287.1 5.5 %copy-start.6 = (bf16[320,1120]{1,0:T(8,128)(2,1)S(1)}, bf16[320,1120]{1,0:T(8,128)(2,1)}, u32[]{:S(2)}) copy-start(bf16[320,1120]{1,0:T(8,128)(2,1)} %get-tuple-element.21) | copy-start | bytes 2150404
  292.6 1.7 copy-start.1
  292.6 3.1 %copy-start.3 = (bf16[2,128,1120]{2,1,0:T(8,128)(2,1)S(1)}, bf16[2,128,1120]{2,1,0:T(8,128)(2,1)}, u32[]{:S(2)}) copy-start(bf16[2,128,1120]{2,1,0:T(8,128)(2,1)} %get-tuple-element.44) | copy-start | bytes 1720324
